TPU v7x, 32 devices: a whole 2x2x4 slice. The times are simulated.
32 devices in a mesh: az: 2 (over core), row: 16 (over z, y, x).
Axes of the slice: x: 2, y: 2, z: 4, core: 2. Of those that a mesh axis runs over, the one named last changes fastest.
Arguments:
- echoes: bfloat16 [2, 768, 16384], P(None, ('az', 'row')), may hold values from -6 to 6
- scaling_phase: bfloat16 [512, 16384], P('row'), may hold values from -3.140625 to 3.140625
- range_phase: bfloat16 [512, 16384], P('row'), may hold values from -3.140625 to 3.140625
- residual_phase: bfloat16 [512, 16384], P('row'), may hold values from -3.140625 to 3.140625
Outputs:
- focused: bfloat16 [2, 768, 16384], P(None, 'az', 'row')
All inputs are finite; a program needn't handle non-finite values.
Results may differ from a plain program's by a relative error of at most 0.014.
Values may be sent and summed in bfloat16 or wider, within the bound.
A program may use at most 64 MiB of HBM per device.

v0:
```python
import functools
import math

import jax
import jax.numpy as jnp
import ml_dtypes
import numpy as np
from jax import lax
from jax.experimental import pallas as pl
from jax.experimental.pallas import tpu as pltpu
from jax.sharding import PartitionSpec as P

SECTION_A = 128
MARGIN = 128
FG = 8
MESH = pl.DeviceIdType.MESH
F32 = jnp.float32
BF16 = jnp.bfloat16


def dft_table(length, rotation):
    indices = np.arange(length)
    angles = (indices[:, None] * indices[None, :] % length) * (2.0 * math.pi / length)
    factor = 1.0 / math.sqrt(length)
    rounded = lambda values: values.astype(ml_dtypes.bfloat16).astype(np.float32)
    return rounded(np.cos(angles) * factor), rounded(rotation * np.sin(angles) * factor)


def tables(n, pulses, rows, margin_blocks, block, per_device):
    length = block + MARGIN
    groups = per_device // FG
    freq = np.arange(length).reshape(n, groups, FG).transpose(1, 0, 2)
    real, imag = dft_table(length, -1.0)
    sources = n + margin_blocks
    forward = np.zeros((groups, n, 2, FG, sources, rows), np.float32)
    for s in range(sources):
        first = s * pulses if s < n else block + (s - n) * pulses
        count = min(pulses, (block if s < n else length) - first)
        m = first + np.arange(count)
        wr = real[m][:, freq].transpose(1, 2, 3, 0)
        wi = imag[m][:, freq].transpose(1, 2, 3, 0)
        forward[:, :, 0, :, s, :count] = wr
        forward[:, :, 0, :, s, pulses : pulses + count] = -wi
        forward[:, :, 1, :, s, :count] = wi
        forward[:, :, 1, :, s, pulses : pulses + count] = wr
    forward = forward.reshape(groups, n * 2 * FG, sources * rows)
    real, imag = dft_table(length, 1.0)
    backward = np.zeros((2, block, groups, n, 2, FG), np.float32)
    wr, wi = real[:block][:, freq], imag[:block][:, freq]
    backward[0, :, :, :, 0], backward[0, :, :, :, 1] = wr, -wi
    backward[1, :, :, :, 0], backward[1, :, :, :, 1] = wi, wr
    backward = backward.reshape(2 * block, groups * n * 2 * FG)
    sections = []
    for rotation in (-1.0, 1.0):
        real, imag = dft_table(SECTION_A, rotation)
        sections.append(np.block([[real, -imag], [imag, real]]))
        sections.append(np.block([[real, imag], [-imag, real]]))
    index = np.arange(SECTION_A)
    angles = index[:, None] * index[None, :] * (2.0 * math.pi / SECTION_A**2)
    twiddle = np.stack([np.cos(angles), np.sin(angles)]).astype(np.float32)
    as_bf16 = lambda values: values.astype(ml_dtypes.bfloat16)
    return as_bf16(forward), as_bf16(backward), as_bf16(np.stack(sections)), twiddle


def cos_sin(x):
    h = x * 0.5
    q = h * h
    s = 1.0 / 362880.0
    for c in (-1.0 / 5040.0, 1.0 / 120.0, -1.0 / 6.0, 1.0):
        s = s * q + c
    s = s * h
    k = -1.0 / 3628800.0
    for c in (1.0 / 40320.0, -1.0 / 720.0, 1.0 / 24.0, -0.5, 1.0):
        k = k * q + c
    return 1.0 - 2.0 * s * s, 2.0 * s * k


def kernel(
    n, n_az, margin_blocks, groups, rc,
    echoes, scaling, rng, residual, forward, backward, sections, twiddle,
    out,
    recv1, spec, recv2, send3, recv3, ph, sc_t, rg_t, rs_t, xs,
    s1, r1, s2, r2, l2, s3, r3, l3, pm, ms, mr,
):
    a, me = lax.axis_index("az"), lax.axis_index("row")
    lane_tiles = rc // 128
    order = sorted(range(1, n), key=lambda i: abs(i - n // 2))

    def peer(i):
        return lax.rem(me + i, n)

    barrier = pltpu.get_barrier_semaphore()
    for i in range(1, n):
        pl.semaphore_signal(barrier, inc=1, device_id={"row": peer(i)}, device_id_type=MESH)

    steps = sorted({1, n_az - 1})
    for step in steps:
        beside = lax.rem(a + step, n_az)
        pl.semaphore_signal(barrier, inc=1, device_id={"az": beside}, device_id_type=MESH)
    pl.semaphore_wait(barrier, n - 1 + len(steps))

    def columns(d):
        return pl.ds(pl.multiple_of(d * rc, 128), rc)

    for i in order:
        d = peer(i)
        pltpu.make_async_remote_copy(
            src_ref=echoes.at[:, columns(d)], dst_ref=recv1.at[me], send_sem=s1,
            recv_sem=r1.at[me], device_id={"row": d}, device_id_type=MESH,
        ).start()
    pltpu.make_async_copy(echoes.at[:, columns(me)], recv1.at[me], r1.at[me]).start()
    for k, phase in enumerate((scaling, rng, residual)):
        pltpu.make_async_copy(phase, ph.at[k], pm.at[k]).start()

    @pl.when(a == n_az - 1)
    def _():
        for j in range(margin_blocks):
            recv1[n + j] = jnp.zeros(recv1.shape[1:], BF16)

    for k, phase in enumerate((scaling, rng, residual)):
        pltpu.make_async_copy(phase, ph.at[k], pm.at[k]).wait()
    for k, table in ((0, sc_t), (2, rs_t)):
        for pair in range(groups // 2):

            def natural(d, carry, k=k, table=table, pair=pair):
                x = ph[k, pl.ds(pair * 2 * FG, 2 * FG), columns(d)].astype(F32)
                c, s = cos_sin(x)
                for h in range(2):
                    table[2 * pair + h, d, 0] = c[h * FG : (h + 1) * FG]
                    table[2 * pair + h, d, 1] = s[h * FG : (h + 1) * FG]
                return carry

            lax.fori_loop(0, n, natural, 0)
    for pair in range(groups // 2):

        def spread(d, carry, pair=pair):
            x = ph[1, pl.ds(pair * 2 * FG, 2 * FG), columns(d)].astype(F32)
            for j in range(lane_tiles):
                at = pl.ds(pl.multiple_of((d * lane_tiles + j) * FG, FG), FG)
                for h in range(2):
                    xs[h, at, :] = x[h * FG : (h + 1) * FG, j * 128 : (j + 1) * 128]
            return carry

        lax.fori_loop(0, n, spread, 0)
        for h in range(2):
            for f in range(FG):
                c, s = cos_sin(xs[h, pl.ds(f, 128, stride=FG), :].T)
                rg_t[2 * pair + h, f, 0] = c
                rg_t[2 * pair + h, f, 1] = s

    def arrived(s):
        pltpu.make_async_copy(echoes.at[:, pl.ds(0, rc)], recv1.at[s], r1.at[s]).wait()

    def margin_copy():
        return pltpu.make_async_remote_copy(
            src_ref=recv1.at[pl.ds(0, margin_blocks)],
            dst_ref=recv1.at[pl.ds(n, margin_blocks)],
            send_sem=ms, recv_sem=mr,
            device_id={"az": a - 1}, device_id_type=MESH,
        )

    for s in range(margin_blocks):
        arrived(s)

    @pl.when(a > 0)
    def _():
        margin_copy().start()

    for s in range(margin_blocks, n):
        arrived(s)

    @pl.when(a < n_az - 1)
    def _():
        pltpu.make_async_copy(
            recv1.at[pl.ds(0, margin_blocks)], recv1.at[pl.ds(n, margin_blocks)], mr
        ).wait()

    def send_group(source, target, g, send_sem, recv_sem, local_sem):
        for i in order:
            d = peer(i)
            pltpu.make_async_remote_copy(
                src_ref=source.at[g, d], dst_ref=target.at[g, me], send_sem=send_sem.at[g],
                recv_sem=recv_sem.at[g], device_id={"row": d}, device_id_type=MESH,
            ).start()
        pltpu.make_async_copy(source.at[g, me], target.at[g, me], local_sem.at[g]).start()

    def group_wait(source, target, g, sem):
        some = pl.ds(0, n - 1)
        pltpu.make_async_copy(source.at[g, some], target.at[g, some], sem.at[g]).wait()

    def group_arrived(source, target, g, recv_sem, local_sem):
        group_wait(source, target, g, recv_sem)
        pltpu.make_async_copy(source.at[g, me], target.at[g, me], local_sem.at[g]).wait()

    depth = recv1.shape[0] * recv1.shape[1]

    def azimuth(g, carry):
        total = jnp.dot(forward[g], recv1[...].reshape(depth, rc), preferred_element_type=F32)
        spec[g] = total.astype(BF16).reshape(n, 2 * FG, rc)
        send_group(spec, recv2, g, s2, r2, l2)
        return carry

    lax.fori_loop(0, groups, azimuth, 0)

    def part(values, f):
        return values[:, f * 128 : (f + 1) * 128]

    def range_group(g, carry):
        group_arrived(spec, recv2, g, r2, l2)

        def scale(d, inner):
            block = recv2[g, d].astype(F32)
            re, im = block[:FG], block[FG:]
            c, s = sc_t[g, d, 0], sc_t[g, d, 1]
            x, y = re * c - im * s, re * s + im * c
            for j in range(lane_tiles):
                at = pl.ds(pl.multiple_of((d * lane_tiles + j) * FG, FG), FG)
                xs[0, at, :] = part(x, j)
                xs[1, at, :] = part(y, j)
            return inner

        lax.fori_loop(0, n, scale, 0)
        tc, ts = twiddle[0], twiddle[1]
        v = jnp.concatenate(
            [
                jnp.concatenate(
                    [xs[c, pl.ds(f, 128, stride=FG), :].astype(BF16) for f in range(FG)], axis=1
                )
                for c in range(2)
            ],
            axis=0,
        )
        y = jnp.dot(sections[0], v, preferred_element_type=F32)
        half = []
        for f in range(FG):
            re, im = part(y[:128], f), part(y[128:], f)
            half.append(jnp.concatenate([re * tc + im * ts, im * tc - re * ts], axis=1).astype(BF16))
        z = jnp.dot(jnp.concatenate(half, axis=0), sections[1], preferred_element_type=F32)
        squeezed = []
        for f in range(FG):
            rows = z[f * 128 : (f + 1) * 128]
            re, im = rows[:, :128], rows[:, 128:]
            c, s = rg_t[g, f, 0], rg_t[g, f, 1]
            squeezed.append(jnp.concatenate([re * c - im * s, re * s + im * c], axis=1).astype(BF16))
        u = jnp.dot(jnp.concatenate(squeezed, axis=0), sections[3], preferred_element_type=F32)
        reals, imags = [], []
        for f in range(FG):
            rows = u[f * 128 : (f + 1) * 128]
            re, im = rows[:, :128], rows[:, 128:]
            reals.append((re * tc - im * ts).astype(BF16))
            imags.append((re * ts + im * tc).astype(BF16))
        q = jnp.concatenate(
            [jnp.concatenate(reals, axis=1), jnp.concatenate(imags, axis=1)], axis=0
        )
        w = jnp.dot(sections[2], q, preferred_element_type=F32)
        for f in range(FG):
            xs[0, pl.ds(f, 128, stride=FG), :] = part(w[:128], f)
            xs[1, pl.ds(f, 128, stride=FG), :] = part(w[128:], f)

        def finish(d, inner):
            res, ims = [], []
            for j in range(lane_tiles):
                at = pl.ds(pl.multiple_of((d * lane_tiles + j) * FG, FG), FG)
                res.append(xs[0, at, :])
                ims.append(xs[1, at, :])
            re, im = jnp.concatenate(res, axis=1), jnp.concatenate(ims, axis=1)
            c, s = rs_t[g, d, 0], rs_t[g, d, 1]
            send3[g, d] = jnp.concatenate([re * c - im * s, re * s + im * c], axis=0).astype(BF16)
            return inner

        lax.fori_loop(0, n, finish, 0)
        send_group(send3, recv3, g, s3, r3, l3)
        return carry

    lax.fori_loop(0, groups, range_group, 0)

    for g in range(groups):
        group_arrived(send3, recv3, g, r3, l3)
    out[...] = jnp.dot(
        backward[...], recv3[...].reshape(groups * n * 2 * FG, rc), preferred_element_type=F32
    ).astype(BF16)

    for g in range(groups):
        group_wait(spec, recv2, g, s2)
        group_wait(send3, recv3, g, s3)
    some = pl.ds(0, n - 1)
    pltpu.make_async_copy(recv1.at[some], recv1.at[some], s1).wait()

    @pl.when(a > 0)
    def _():
        margin_copy().wait_send()


def on_device(n_az, n, echoes, scaling_phase, range_phase, residual_phase):
    _, pulses, length = echoes.shape
    per_device = scaling_phase.shape[0]
    rc = length // n
    block = pulses * n
    rows = -(-2 * pulses // 16) * 16
    margin_blocks = -(-MARGIN // pulses)
    groups = per_device // FG
    stacked = echoes.reshape(2 * pulses, length)
    if rows > 2 * pulses:
        stacked = jnp.pad(stacked, ((0, rows - 2 * pulses), (0, 0)))
    forward, backward, sections, twiddle = tables(n, pulses, rows, margin_blocks, block, per_device)
    anywhere = pl.BlockSpec(memory_space=pl.ANY)
    vmem = pl.BlockSpec(memory_space=pltpu.VMEM)
    exchange = pltpu.VMEM((groups, n, 2 * FG, rc), BF16)
    dma = pltpu.SemaphoreType.DMA
    result = pl.pallas_call(
        functools.partial(kernel, n, n_az, margin_blocks, groups, rc),
        out_shape=jax.ShapeDtypeStruct((2 * block, rc), BF16),
        in_specs=[anywhere] * 4 + [vmem] * 4,
        out_specs=vmem,
        scratch_shapes=[
            pltpu.VMEM((n + margin_blocks, rows, rc), BF16),
            exchange, exchange, exchange, exchange,
            pltpu.VMEM((3, per_device, length), BF16),
            pltpu.VMEM((groups, n, 2, FG, rc), F32),
            pltpu.VMEM((groups, FG, 2, 128, 128), F32),
            pltpu.VMEM((groups, n, 2, FG, rc), F32),
            pltpu.VMEM((2, 128 * FG, 128), F32),
            dma, dma((n,)), dma((groups,)), dma((groups,)), dma((groups,)),
            dma((groups,)), dma((groups,)), dma((groups,)), dma((3,)), dma, dma,
        ],
        compiler_params=pltpu.CompilerParams(
            collective_id=0, has_side_effects=True, vmem_limit_bytes=56 * 1024 * 1024
        ),
    )(
        stacked, scaling_phase, range_phase, residual_phase,
        jnp.asarray(forward), jnp.asarray(backward), jnp.asarray(sections), jnp.asarray(twiddle),
    )
    return result.reshape(2, block, rc)


def solution(mesh):
    placed = (P(None, ("az", "row"), None), P("row", None), P("row", None), P("row", None))
    return jax.shard_map(
        functools.partial(on_device, mesh.shape["az"], mesh.shape["row"]),
        mesh=mesh, in_specs=placed, out_specs=P(None, "az", "row"), check_vma=False,
    )
```

profile of v0, /device:TPU:0, one launch (start us, length us, event | category | flops | bytes accessed | tf_op | source)
XLA Modules:
  0.0 139.5 jit_solution(14592748336964381413)
XLA Ops:
  0.0 136.8 %shard_map.82 = bf16[768,1024]{1,0:T(8,128)(2,1)} custom-call(bf16[48,16384]{1,0:T(8,128)(2,1)} %bitcast.3, bf16[32,16384]{1,0:T(8,128)(2,1)} %scaling.1, bf16[32,16384]{1,0:T(8,128)(2,1)} %rng.1, bf16[32,16384]{1,0:T(8,128)(2,1)} %residual.1, bf16[4,256,1056]{2,1,0:T(8,128)(2,1)} %constant.8.clone.forward, bf16[768,1024]{1,0:T(8,128)(2,1)} %constant.9.clone.backward, ...), custom_call_target="tpu_custom_call" | custom-call | tf_op jit(solution)/shard_map/pallas_call | solution.py:310
  136.8 2.7 %copy.10 = bf16[2,384,1024]{2,1,0:T(8,128)(2,1)} copy(bf16[2,384,1024]{2,1,0:T(8,128)(2,1)} %bitcast.2) | data formatting | bytes 3145728
where the time goes:
time: 141 us; the launch traced here: 139 us
  Pallas kernels  137 us (97%)
  local copies, waits for them, and re-layouts  2.67 us (2%)
    pallas_call x1, Pallas kernels, on_device(): pl.pallas_call(functools.partial(kernel, n, n_az, margin_blocks, groups,...  137 us

commit v1 on v0

--- a/solution.py
+++ b/solution.py
@@ -13,6 +13,7 @@
 SECTION_A = 128
 MARGIN = 128
 FG = 8
+CHUNKS = 2
 MESH = pl.DeviceIdType.MESH
 F32 = jnp.float32
 BF16 = jnp.bfloat16
@@ -49,7 +50,7 @@
     wr, wi = real[:block][:, freq], imag[:block][:, freq]
     backward[0, :, :, :, 0], backward[0, :, :, :, 1] = wr, -wi
     backward[1, :, :, :, 0], backward[1, :, :, :, 1] = wi, wr
-    backward = backward.reshape(2 * block, groups * n * 2 * FG)
+    backward = backward.reshape(2 * block, groups, n * 2 * FG).transpose(1, 0, 2)
     sections = []
     for rotation in (-1.0, 1.0):
         real, imag = dft_table(SECTION_A, rotation)
@@ -77,20 +78,27 @@
 
 def kernel(
     n, n_az, margin_blocks, groups, rc,
-    echoes, scaling, rng, residual, forward, backward, sections, twiddle,
+    echoes, scaling, rng, residual, forward_in, backward_in, sections_in, twiddle_in,
     out,
-    recv1, spec, recv2, send3, recv3, ph, sc_t, rg_t, rs_t, xs,
-    s1, r1, s2, r2, l2, s3, r3, l3, pm, ms, mr,
+    recv1, spec, recv2, send3, recv3, ph, sc_t, rg_t, rs_t, xs, total_back,
+    forward, backward, sections, twiddle,
+    s1, r1, s2, r2, l2, s3, r3, l3, pm, ms, mr, tm,
 ):
     a, me = lax.axis_index("az"), lax.axis_index("row")
-    lane_tiles = rc // 128
-    order = sorted(range(1, n), key=lambda i: abs(i - n // 2))
-
-    def peer(i):
-        return lax.rem(me + i, n)
+    lane_tiles, cw = rc // 128, rc // CHUNKS
+    half_row = n // 2
+    side, place = lax.div(me, half_row), lax.rem(me, half_row)
+    order = [(1, 0)]
+    for i in range(1, half_row):
+        order += [(0, i), (1, i)]
+
+    def peer(partner):
+        other, i = partner
+        there = 1 - side if other else side
+        return there * half_row + lax.rem(place + i, half_row)
 
     barrier = pltpu.get_barrier_semaphore()
-    for i in range(1, n):
+    for i in order:
         pl.semaphore_signal(barrier, inc=1, device_id={"row": peer(i)}, device_id_type=MESH)
 
     steps = sorted({1, n_az - 1})
@@ -102,114 +110,148 @@
     def columns(d):
         return pl.ds(pl.multiple_of(d * rc, 128), rc)
 
-    for i in order:
-        d = peer(i)
-        pltpu.make_async_remote_copy(
-            src_ref=echoes.at[:, columns(d)], dst_ref=recv1.at[me], send_sem=s1,
-            recv_sem=r1.at[me], device_id={"row": d}, device_id_type=MESH,
-        ).start()
-    pltpu.make_async_copy(echoes.at[:, columns(me)], recv1.at[me], r1.at[me]).start()
-    for k, phase in enumerate((scaling, rng, residual)):
-        pltpu.make_async_copy(phase, ph.at[k], pm.at[k]).start()
-
-    @pl.when(a == n_az - 1)
-    def _():
-        for j in range(margin_blocks):
-            recv1[n + j] = jnp.zeros(recv1.shape[1:], BF16)
-
-    for k, phase in enumerate((scaling, rng, residual)):
-        pltpu.make_async_copy(phase, ph.at[k], pm.at[k]).wait()
-    for k, table in ((0, sc_t), (2, rs_t)):
-        for pair in range(groups // 2):
-
-            def natural(d, carry, k=k, table=table, pair=pair):
-                x = ph[k, pl.ds(pair * 2 * FG, 2 * FG), columns(d)].astype(F32)
-                c, s = cos_sin(x)
-                for h in range(2):
-                    table[2 * pair + h, d, 0] = c[h * FG : (h + 1) * FG]
-                    table[2 * pair + h, d, 1] = s[h * FG : (h + 1) * FG]
-                return carry
-
-            lax.fori_loop(0, n, natural, 0)
-    for pair in range(groups // 2):
-
-        def spread(d, carry, pair=pair):
-            x = ph[1, pl.ds(pair * 2 * FG, 2 * FG), columns(d)].astype(F32)
-            for j in range(lane_tiles):
-                at = pl.ds(pl.multiple_of((d * lane_tiles + j) * FG, FG), FG)
-                for h in range(2):
-                    xs[h, at, :] = x[h * FG : (h + 1) * FG, j * 128 : (j + 1) * 128]
-            return carry
-
-        lax.fori_loop(0, n, spread, 0)
-        for h in range(2):
-            for f in range(FG):
-                c, s = cos_sin(xs[h, pl.ds(f, 128, stride=FG), :].T)
-                rg_t[2 * pair + h, f, 0] = c
-                rg_t[2 * pair + h, f, 1] = s
-
-    def arrived(s):
-        pltpu.make_async_copy(echoes.at[:, pl.ds(0, rc)], recv1.at[s], r1.at[s]).wait()
-
-    def margin_copy():
-        return pltpu.make_async_remote_copy(
-            src_ref=recv1.at[pl.ds(0, margin_blocks)],
-            dst_ref=recv1.at[pl.ds(n, margin_blocks)],
-            send_sem=ms, recv_sem=mr,
-            device_id={"az": a - 1}, device_id_type=MESH,
-        )
-
-    for s in range(margin_blocks):
-        arrived(s)
-
-    @pl.when(a > 0)
-    def _():
-        margin_copy().start()
-
-    for s in range(margin_blocks, n):
-        arrived(s)
-
-    @pl.when(a < n_az - 1)
-    def _():
-        pltpu.make_async_copy(
-            recv1.at[pl.ds(0, margin_blocks)], recv1.at[pl.ds(n, margin_blocks)], mr
-        ).wait()
-
-    def send_group(source, target, g, send_sem, recv_sem, local_sem):
+    def chunk_columns(d, ch):
+        return pl.ds(pl.multiple_of(d * rc + ch * cw, 128), cw)
+
+    for ch in range(CHUNKS):
         for i in order:
             d = peer(i)
             pltpu.make_async_remote_copy(
-                src_ref=source.at[g, d], dst_ref=target.at[g, me], send_sem=send_sem.at[g],
-                recv_sem=recv_sem.at[g], device_id={"row": d}, device_id_type=MESH,
+                src_ref=echoes.at[:, chunk_columns(d, ch)], dst_ref=recv1.at[ch, me],
+                send_sem=s1.at[ch], recv_sem=r1.at[ch, me],
+                device_id={"row": d}, device_id_type=MESH,
             ).start()
-        pltpu.make_async_copy(source.at[g, me], target.at[g, me], local_sem.at[g]).start()
-
-    def group_wait(source, target, g, sem):
+        pltpu.make_async_copy(
+            echoes.at[:, chunk_columns(me, ch)], recv1.at[ch, me], r1.at[ch, me]
+        ).start()
+    loads = [pltpu.make_async_copy(p, ph.at[k], pm.at[k]) for k, p in enumerate((scaling, rng, residual))]
+    fixed = ((forward_in, forward), (twiddle_in, twiddle), (sections_in, sections), (backward_in, backward))
+    loads += [pltpu.make_async_copy(x, y, tm.at[k]) for k, (x, y) in enumerate(fixed)]
+    for k in (0, 3, 1, 2, 4, 5, 6):
+        loads[k].start()
+
+    @pl.when(a == n_az - 1)
+    def _():
+        for ch in range(CHUNKS):
+            for j in range(margin_blocks):
+                recv1[ch, n + j] = jnp.zeros(recv1.shape[2:], BF16)
+
+    def natural_table(k, table):
+        loads[k].wait()
+
+        def natural(step, carry):
+            pair, d = lax.div(step, n), lax.rem(step, n)
+            rows = pl.ds(pl.multiple_of(pair * 2 * FG, 2 * FG), 2 * FG)
+            c, s = cos_sin(ph[k, rows, columns(d)].astype(F32))
+            for h in range(2):
+                table[2 * pair + h, d, 0] = c[h * FG : (h + 1) * FG]
+                table[2 * pair + h, d, 1] = s[h * FG : (h + 1) * FG]
+            return carry
+
+        lax.fori_loop(0, n * (groups // 2), natural, 0)
+
+    def turned_table():
+        loads[1].wait()
+
+        def turn(pair, carry):
+            rows = pl.ds(pl.multiple_of(pair * 2 * FG, 2 * FG), 2 * FG)
+
+            def spread(d, inner):
+                x = ph[1, rows, columns(d)].astype(F32)
+                for j in range(lane_tiles):
+                    at = pl.ds(pl.multiple_of((d * lane_tiles + j) * FG, FG), FG)
+                    for h in range(2):
+                        xs[h, at, :] = x[h * FG : (h + 1) * FG, j * 128 : (j + 1) * 128]
+                return inner
+
+            lax.fori_loop(0, n, spread, 0)
+            for h in range(2):
+                for f in range(FG):
+                    c, s = cos_sin(xs[h, pl.ds(f, 128, stride=FG), :].T)
+                    rg_t[2 * pair + h, f, 0] = c
+                    rg_t[2 * pair + h, f, 1] = s
+            return carry
+
+        lax.fori_loop(0, groups // 2, turn, 0)
+
+    def arrived(ch, s):
+        pltpu.make_async_copy(echoes.at[:, pl.ds(0, cw)], recv1.at[ch, s], r1.at[ch, s]).wait()
+
+    def margin_copy(ch):
+        return pltpu.make_async_remote_copy(
+            src_ref=recv1.at[ch, pl.ds(0, margin_blocks)],
+            dst_ref=recv1.at[ch, pl.ds(n, margin_blocks)],
+            send_sem=ms.at[ch], recv_sem=mr.at[ch],
+            device_id={"az": a - 1}, device_id_type=MESH,
+        )
+
+    def send_group(source, target, at, send_sem, recv_sem, local_sem):
+        for i in order:
+            d = peer(i)
+            pltpu.make_async_remote_copy(
+                src_ref=source.at[(*at, d)], dst_ref=target.at[(*at, me)], send_sem=send_sem.at[at],
+                recv_sem=recv_sem.at[at], device_id={"row": d}, device_id_type=MESH,
+            ).start()
+        pltpu.make_async_copy(
+            source.at[(*at, me)], target.at[(*at, me)], local_sem.at[at]
+        ).start()
+
+    def group_wait(source, target, at, sem):
         some = pl.ds(0, n - 1)
-        pltpu.make_async_copy(source.at[g, some], target.at[g, some], sem.at[g]).wait()
-
-    def group_arrived(source, target, g, recv_sem, local_sem):
-        group_wait(source, target, g, recv_sem)
-        pltpu.make_async_copy(source.at[g, me], target.at[g, me], local_sem.at[g]).wait()
-
-    depth = recv1.shape[0] * recv1.shape[1]
-
-    def azimuth(g, carry):
-        total = jnp.dot(forward[g], recv1[...].reshape(depth, rc), preferred_element_type=F32)
-        spec[g] = total.astype(BF16).reshape(n, 2 * FG, rc)
-        send_group(spec, recv2, g, s2, r2, l2)
-        return carry
-
-    lax.fori_loop(0, groups, azimuth, 0)
+        pltpu.make_async_copy(source.at[(*at, some)], target.at[(*at, some)], sem.at[at]).wait()
+
+    def group_arrived(source, target, at, recv_sem, local_sem):
+        group_wait(source, target, at, recv_sem)
+        pltpu.make_async_copy(source.at[(*at, me)], target.at[(*at, me)], local_sem.at[at]).wait()
+
+    depth = recv1.shape[1] * recv1.shape[2]
+
+    def azimuth_chunk(ch):
+        for s in range(margin_blocks):
+            arrived(ch, s)
+
+        @pl.when(a > 0)
+        def _():
+            margin_copy(ch).start()
+
+        for s in range(margin_blocks, n):
+            arrived(ch, s)
+
+        @pl.when(a < n_az - 1)
+        def _():
+            pltpu.make_async_copy(
+                recv1.at[ch, pl.ds(0, margin_blocks)], recv1.at[ch, pl.ds(n, margin_blocks)],
+                mr.at[ch],
+            ).wait()
+
+        def azimuth(g, carry):
+            total = jnp.dot(
+                forward[g], recv1[ch].reshape(depth, cw), preferred_element_type=F32
+            )
+            spec[g, ch] = total.astype(BF16).reshape(n, 2 * FG, cw)
+            send_group(spec, recv2, (g, ch), s2, r2, l2)
+            return carry
+
+        lax.fori_loop(0, groups, azimuth, 0)
+
+    natural_table(0, sc_t)
+    loads[3].wait()
+    azimuth_chunk(0)
+    turned_table()
+    azimuth_chunk(1)
+    natural_table(2, rs_t)
+    for k in (4, 5, 6):
+        loads[k].wait()
 
     def part(values, f):
         return values[:, f * 128 : (f + 1) * 128]
 
     def range_group(g, carry):
-        group_arrived(spec, recv2, g, r2, l2)
+        for ch in range(CHUNKS):
+            group_arrived(spec, recv2, (g, ch), r2, l2)
 
         def scale(d, inner):
-            block = recv2[g, d].astype(F32)
+            block = jnp.concatenate([recv2[g, ch, d] for ch in range(CHUNKS)], axis=1).astype(F32)
             re, im = block[:FG], block[FG:]
             c, s = sc_t[g, d, 0], sc_t[g, d, 1]
             x, y = re * c - im * s, re * s + im * c
@@ -269,26 +311,34 @@
             return inner
 
         lax.fori_loop(0, n, finish, 0)
-        send_group(send3, recv3, g, s3, r3, l3)
+        send_group(send3, recv3, (g,), s3, r3, l3)
         return carry
 
     lax.fori_loop(0, groups, range_group, 0)
 
     for g in range(groups):
-        group_arrived(send3, recv3, g, r3, l3)
-    out[...] = jnp.dot(
-        backward[...], recv3[...].reshape(groups * n * 2 * FG, rc), preferred_element_type=F32
-    ).astype(BF16)
+        group_arrived(send3, recv3, (g,), r3, l3)
+        term = jnp.dot(
+            backward[g], recv3[g].reshape(n * 2 * FG, rc), preferred_element_type=F32
+        )
+        if g > 0:
+            term = total_back[...] + term
+        if g < groups - 1:
+            total_back[...] = term
+        else:
+            out[...] = term.astype(BF16)
 
     for g in range(groups):
-        group_wait(spec, recv2, g, s2)
-        group_wait(send3, recv3, g, s3)
+        for ch in range(CHUNKS):
+            group_wait(spec, recv2, (g, ch), s2)
+        group_wait(send3, recv3, (g,), s3)
     some = pl.ds(0, n - 1)
-    pltpu.make_async_copy(recv1.at[some], recv1.at[some], s1).wait()
-
-    @pl.when(a > 0)
-    def _():
-        margin_copy().wait_send()
+    for ch in range(CHUNKS):
+        pltpu.make_async_copy(recv1.at[ch, some], recv1.at[ch, some], s1.at[ch]).wait()
+
+        @pl.when(a > 0)
+        def _(ch=ch):
+            margin_copy(ch).wait_send()
 
 
 def on_device(n_az, n, echoes, scaling_phase, range_phase, residual_phase):
@@ -306,22 +356,27 @@
     anywhere = pl.BlockSpec(memory_space=pl.ANY)
     vmem = pl.BlockSpec(memory_space=pltpu.VMEM)
     exchange = pltpu.VMEM((groups, n, 2 * FG, rc), BF16)
+    chunked = pltpu.VMEM((groups, CHUNKS, n, 2 * FG, rc // CHUNKS), BF16)
     dma = pltpu.SemaphoreType.DMA
     result = pl.pallas_call(
         functools.partial(kernel, n, n_az, margin_blocks, groups, rc),
         out_shape=jax.ShapeDtypeStruct((2 * block, rc), BF16),
-        in_specs=[anywhere] * 4 + [vmem] * 4,
+        in_specs=[anywhere] * 8,
         out_specs=vmem,
         scratch_shapes=[
-            pltpu.VMEM((n + margin_blocks, rows, rc), BF16),
-            exchange, exchange, exchange, exchange,
+            pltpu.VMEM((CHUNKS, n + margin_blocks, rows, rc // CHUNKS), BF16),
+            chunked, chunked, exchange, exchange,
             pltpu.VMEM((3, per_device, length), BF16),
             pltpu.VMEM((groups, n, 2, FG, rc), F32),
             pltpu.VMEM((groups, FG, 2, 128, 128), F32),
             pltpu.VMEM((groups, n, 2, FG, rc), F32),
             pltpu.VMEM((2, 128 * FG, 128), F32),
-            dma, dma((n,)), dma((groups,)), dma((groups,)), dma((groups,)),
-            dma((groups,)), dma((groups,)), dma((groups,)), dma((3,)), dma, dma,
+            pltpu.VMEM((2 * block, rc), F32),
+            *[pltpu.VMEM(t.shape, t.dtype) for t in (forward, backward, sections, twiddle)],
+            dma((CHUNKS,)), dma((CHUNKS, n)),
+            dma((groups, CHUNKS)), dma((groups, CHUNKS)), dma((groups, CHUNKS)),
+            dma((groups,)), dma((groups,)), dma((groups,)),
+            dma((3,)), dma((CHUNKS,)), dma((CHUNKS,)), dma((4,)),
         ],
         compiler_params=pltpu.CompilerParams(
             collective_id=0, has_side_effects=True, vmem_limit_bytes=56 * 1024 * 1024

time: 141 us -> 137 us (0.972); the launches traced: 139 us -> 137 us
  Pallas kernels: 137 us -> 134 us
    pallas_call x1, Pallas kernels: 137 us -> 134 us  [on_device(): pl.pallas_call(functools.partial(kernel, n, n_az, margin_blocks, groups,...]
where the time goes in v1:
time: 137 us
  Pallas kernels  134 us (98%)
  local copies, waits for them, and re-layouts  2.67 us (2%)
    pallas_call x1, Pallas kernels, on_device(): pl.pallas_call(functools.partial(kernel, n, n_az, margin_blocks, groups,...  134 us

profile of v1, /device:TPU:0, one launch (start us, length us, event | category | flops | bytes accessed | tf_op | source)
XLA Modules:
  0.0 137.0 jit_solution(12482203103966397700)
XLA Ops:
  0.0 134.3 %shard_map.82 = bf16[768,1024]{1,0:T(8,128)(2,1)} custom-call(bf16[48,16384]{1,0:T(8,128)(2,1)} %bitcast.3, bf16[32,16384]{1,0:T(8,128)(2,1)} %scaling.1, bf16[32,16384]{1,0:T(8,128)(2,1)} %rng.1, bf16[32,16384]{1,0:T(8,128)(2,1)} %residual.1, bf16[4,256,1056]{2,1,0:T(8,128)(2,1)} %constant.8.clone.forward_in, ...), custom_call_target="tpu_custom_call" | custom-call | tf_op jit(solution)/shard_map/pallas_call | solution.py:361
  134.3 2.7 %copy.10 = bf16[2,384,1024]{2,1,0:T(8,128)(2,1)} copy(bf16[2,384,1024]{2,1,0:T(8,128)(2,1)} %bitcast.2) | data formatting | bytes 3145728

commit v2 on v1

--- a/solution.py
+++ b/solution.py
@@ -13,7 +13,6 @@
 SECTION_A = 128
 MARGIN = 128
 FG = 8
-CHUNKS = 2
 MESH = pl.DeviceIdType.MESH
 F32 = jnp.float32
 BF16 = jnp.bfloat16
@@ -80,17 +79,18 @@
     n, n_az, margin_blocks, groups, rc,
     echoes, scaling, rng, residual, forward_in, backward_in, sections_in, twiddle_in,
     out,
-    recv1, spec, recv2, send3, recv3, ph, sc_t, rg_t, rs_t, xs, total_back,
+    wide, narrow, spec_wide, recv_wide, spec, recv2, send3, recv3, ph, sc_t, rg_t, rs_t, xs, total_back,
     forward, backward, sections, twiddle,
-    s1, r1, s2, r2, l2, s3, r3, l3, pm, ms, mr, tm,
+    s1, r1, sw, rw, lw, s2, r2, l2, s3, r3, l3, pm, ms, mr, tm,
 ):
     a, me = lax.axis_index("az"), lax.axis_index("row")
-    lane_tiles, cw = rc // 128, rc // CHUNKS
+    lane_tiles, w_wide, w_narrow = rc // 128, rc - rc // 4, rc // 4
     half_row = n // 2
     side, place = lax.div(me, half_row), lax.rem(me, half_row)
     order = [(1, 0)]
     for i in range(1, half_row):
         order += [(0, i), (1, i)]
+    near = [(0, i) for i in range(1, half_row)]
 
     def peer(partner):
         other, i = partner
@@ -110,20 +110,28 @@
     def columns(d):
         return pl.ds(pl.multiple_of(d * rc, 128), rc)
 
-    def chunk_columns(d, ch):
-        return pl.ds(pl.multiple_of(d * rc + ch * cw, 128), cw)
-
-    for ch in range(CHUNKS):
+    def piece(d, slot):
+        if slot < 2:
+            start = (lax.rem(d, half_row) + slot * half_row) * rc
+            return pl.ds(pl.multiple_of(start, 128), w_wide)
+        return pl.ds(pl.multiple_of(d * rc + w_wide, 128), w_narrow)
+
+    def landing(slot, at):
+        return wide.at[slot, at] if slot < 2 else narrow.at[at]
+
+    for slots in ((0, 1), (2,)):
         for i in order:
             d = peer(i)
-            pltpu.make_async_remote_copy(
-                src_ref=echoes.at[:, chunk_columns(d, ch)], dst_ref=recv1.at[ch, me],
-                send_sem=s1.at[ch], recv_sem=r1.at[ch, me],
-                device_id={"row": d}, device_id_type=MESH,
+            for slot in slots:
+                pltpu.make_async_remote_copy(
+                    src_ref=echoes.at[:, piece(d, slot)], dst_ref=landing(slot, me),
+                    send_sem=s1.at[slot], recv_sem=r1.at[slot, me],
+                    device_id={"row": d}, device_id_type=MESH,
+                ).start()
+        for slot in slots:
+            pltpu.make_async_copy(
+                echoes.at[:, piece(me, slot)], landing(slot, me), r1.at[slot, me]
             ).start()
-        pltpu.make_async_copy(
-            echoes.at[:, chunk_columns(me, ch)], recv1.at[ch, me], r1.at[ch, me]
-        ).start()
     loads = [pltpu.make_async_copy(p, ph.at[k], pm.at[k]) for k, p in enumerate((scaling, rng, residual))]
     fixed = ((forward_in, forward), (twiddle_in, twiddle), (sections_in, sections), (backward_in, backward))
     loads += [pltpu.make_async_copy(x, y, tm.at[k]) for k, (x, y) in enumerate(fixed)]
@@ -132,9 +140,10 @@
 
     @pl.when(a == n_az - 1)
     def _():
-        for ch in range(CHUNKS):
-            for j in range(margin_blocks):
-                recv1[ch, n + j] = jnp.zeros(recv1.shape[2:], BF16)
+        for j in range(margin_blocks):
+            for slot in range(2):
+                wide[slot, n + j] = jnp.zeros(wide.shape[2:], BF16)
+            narrow[n + j] = jnp.zeros(narrow.shape[1:], BF16)
 
     def natural_table(k, table):
         loads[k].wait()
@@ -174,16 +183,38 @@
 
         lax.fori_loop(0, groups // 2, turn, 0)
 
-    def arrived(ch, s):
-        pltpu.make_async_copy(echoes.at[:, pl.ds(0, cw)], recv1.at[ch, s], r1.at[ch, s]).wait()
-
-    def margin_copy(ch):
+    def margin_copy(slot):
         return pltpu.make_async_remote_copy(
-            src_ref=recv1.at[ch, pl.ds(0, margin_blocks)],
-            dst_ref=recv1.at[ch, pl.ds(n, margin_blocks)],
-            send_sem=ms.at[ch], recv_sem=mr.at[ch],
+            src_ref=landing(slot, pl.ds(0, margin_blocks)),
+            dst_ref=landing(slot, pl.ds(n, margin_blocks)),
+            send_sem=ms.at[slot], recv_sem=mr.at[slot],
             device_id={"az": a - 1}, device_id_type=MESH,
         )
+
+    def pulses_arrived(slots):
+        def arrived(slot, s):
+            pltpu.make_async_copy(
+                echoes.at[:, piece(me, slot)], landing(slot, s), r1.at[slot, s]
+            ).wait()
+
+        for slot in slots:
+            for s in range(margin_blocks):
+                arrived(slot, s)
+
+            @pl.when(a > 0)
+            def _(slot=slot):
+                margin_copy(slot).start()
+
+        for slot in slots:
+            for s in range(margin_blocks, n):
+                arrived(slot, s)
+
+            @pl.when(a < n_az - 1)
+            def _(slot=slot):
+                pltpu.make_async_copy(
+                    landing(slot, pl.ds(0, margin_blocks)), landing(slot, pl.ds(n, margin_blocks)),
+                    mr.at[slot],
+                ).wait()
 
     def send_group(source, target, at, send_sem, recv_sem, local_sem):
         for i in order:
@@ -204,41 +235,58 @@
         group_wait(source, target, at, recv_sem)
         pltpu.make_async_copy(source.at[(*at, me)], target.at[(*at, me)], local_sem.at[at]).wait()
 
-    depth = recv1.shape[1] * recv1.shape[2]
-
-    def azimuth_chunk(ch):
-        for s in range(margin_blocks):
-            arrived(ch, s)
-
-        @pl.when(a > 0)
-        def _():
-            margin_copy(ch).start()
-
-        for s in range(margin_blocks, n):
-            arrived(ch, s)
-
-        @pl.when(a < n_az - 1)
-        def _():
+    depth = narrow.shape[0] * narrow.shape[1]
+    rows_half = half_row * 2 * FG
+
+    def azimuth_wide():
+        pulses_arrived((0, 1))
+        mine = pl.ds(pl.multiple_of(side * rows_half, 16), rows_half)
+        for slot in range(2):
+            total = jnp.dot(
+                forward[:, mine, :].reshape(groups * rows_half, depth),
+                wide[slot].reshape(depth, w_wide), preferred_element_type=F32,
+            )
+            for g in range(groups):
+                rows = total[g * rows_half : (g + 1) * rows_half].astype(BF16)
+                spec_wide[g, :, slot] = rows.reshape(half_row, 2 * FG, w_wide)
+
+        def send(g, carry):
+            for i in near:
+                d = peer(i)
+                pltpu.make_async_remote_copy(
+                    src_ref=spec_wide.at[g, lax.rem(d, half_row)], dst_ref=recv_wide.at[g, place],
+                    send_sem=sw.at[g], recv_sem=rw.at[g],
+                    device_id={"row": d}, device_id_type=MESH,
+                ).start()
             pltpu.make_async_copy(
-                recv1.at[ch, pl.ds(0, margin_blocks)], recv1.at[ch, pl.ds(n, margin_blocks)],
-                mr.at[ch],
-            ).wait()
+                spec_wide.at[g, place], recv_wide.at[g, place], lw.at[g]
+            ).start()
+            return carry
+
+        lax.fori_loop(0, groups, send, 0)
+
+    def wide_wait(g, sem):
+        some = pl.ds(0, half_row - 1)
+        pltpu.make_async_copy(spec_wide.at[g, some], recv_wide.at[g, some], sem.at[g]).wait()
+
+    def azimuth_narrow():
+        pulses_arrived((2,))
 
         def azimuth(g, carry):
             total = jnp.dot(
-                forward[g], recv1[ch].reshape(depth, cw), preferred_element_type=F32
+                forward[g], narrow[...].reshape(depth, w_narrow), preferred_element_type=F32
             )
-            spec[g, ch] = total.astype(BF16).reshape(n, 2 * FG, cw)
-            send_group(spec, recv2, (g, ch), s2, r2, l2)
+            spec[g] = total.astype(BF16).reshape(n, 2 * FG, w_narrow)
+            send_group(spec, recv2, (g,), s2, r2, l2)
             return carry
 
         lax.fori_loop(0, groups, azimuth, 0)
 
     natural_table(0, sc_t)
     loads[3].wait()
-    azimuth_chunk(0)
     turned_table()
-    azimuth_chunk(1)
+    azimuth_wide()
+    azimuth_narrow()
     natural_table(2, rs_t)
     for k in (4, 5, 6):
         loads[k].wait()
@@ -247,11 +295,13 @@
         return values[:, f * 128 : (f + 1) * 128]
 
     def range_group(g, carry):
-        for ch in range(CHUNKS):
-            group_arrived(spec, recv2, (g, ch), r2, l2)
+        wide_wait(g, rw)
+        pltpu.make_async_copy(spec_wide.at[g, place], recv_wide.at[g, place], lw.at[g]).wait()
+        group_arrived(spec, recv2, (g,), r2, l2)
 
         def scale(d, inner):
-            block = jnp.concatenate([recv2[g, ch, d] for ch in range(CHUNKS)], axis=1).astype(F32)
+            first = recv_wide[g, lax.rem(d, half_row), lax.div(d, half_row)]
+            block = jnp.concatenate([first, recv2[g, d]], axis=1).astype(F32)
             re, im = block[:FG], block[FG:]
             c, s = sc_t[g, d, 0], sc_t[g, d, 1]
             x, y = re * c - im * s, re * s + im * c
@@ -329,16 +379,16 @@
             out[...] = term.astype(BF16)
 
     for g in range(groups):
-        for ch in range(CHUNKS):
-            group_wait(spec, recv2, (g, ch), s2)
+        wide_wait(g, sw)
+        group_wait(spec, recv2, (g,), s2)
         group_wait(send3, recv3, (g,), s3)
     some = pl.ds(0, n - 1)
-    for ch in range(CHUNKS):
-        pltpu.make_async_copy(recv1.at[ch, some], recv1.at[ch, some], s1.at[ch]).wait()
+    for slot in range(3):
+        pltpu.make_async_copy(landing(slot, some), landing(slot, some), s1.at[slot]).wait()
 
         @pl.when(a > 0)
-        def _(ch=ch):
-            margin_copy(ch).wait_send()
+        def _(slot=slot):
+            margin_copy(slot).wait_send()
 
 
 def on_device(n_az, n, echoes, scaling_phase, range_phase, residual_phase):
@@ -356,7 +406,11 @@
     anywhere = pl.BlockSpec(memory_space=pl.ANY)
     vmem = pl.BlockSpec(memory_space=pltpu.VMEM)
     exchange = pltpu.VMEM((groups, n, 2 * FG, rc), BF16)
-    chunked = pltpu.VMEM((groups, CHUNKS, n, 2 * FG, rc // CHUNKS), BF16)
+    w_narrow = rc // 4
+    w_wide = rc - w_narrow
+    sources = n + margin_blocks
+    narrow_groups = pltpu.VMEM((groups, n, 2 * FG, w_narrow), BF16)
+    wide_groups = pltpu.VMEM((groups, n // 2, 2, 2 * FG, w_wide), BF16)
     dma = pltpu.SemaphoreType.DMA
     result = pl.pallas_call(
         functools.partial(kernel, n, n_az, margin_blocks, groups, rc),
@@ -364,8 +418,9 @@
         in_specs=[anywhere] * 8,
         out_specs=vmem,
         scratch_shapes=[
-            pltpu.VMEM((CHUNKS, n + margin_blocks, rows, rc // CHUNKS), BF16),
-            chunked, chunked, exchange, exchange,
+            pltpu.VMEM((2, sources, rows, w_wide), BF16),
+            pltpu.VMEM((sources, rows, w_narrow), BF16),
+            wide_groups, wide_groups, narrow_groups, narrow_groups, exchange, exchange,
             pltpu.VMEM((3, per_device, length), BF16),
             pltpu.VMEM((groups, n, 2, FG, rc), F32),
             pltpu.VMEM((groups, FG, 2, 128, 128), F32),
@@ -373,10 +428,8 @@
             pltpu.VMEM((2, 128 * FG, 128), F32),
             pltpu.VMEM((2 * block, rc), F32),
             *[pltpu.VMEM(t.shape, t.dtype) for t in (forward, backward, sections, twiddle)],
-            dma((CHUNKS,)), dma((CHUNKS, n)),
-            dma((groups, CHUNKS)), dma((groups, CHUNKS)), dma((groups, CHUNKS)),
-            dma((groups,)), dma((groups,)), dma((groups,)),
-            dma((3,)), dma((CHUNKS,)), dma((CHUNKS,)), dma((4,)),
+            dma((3,)), dma((3, n)), *[dma((groups,))] * 9,
+            dma((3,)), dma((3,)), dma((3,)), dma((4,)),
         ],
         compiler_params=pltpu.CompilerParams(
             collective_id=0, has_side_effects=True, vmem_limit_bytes=56 * 1024 * 1024

time: 137 us -> 143 us (1.044)
  Pallas kernels: 134 us -> 141 us
    pallas_call x1, Pallas kernels: 134 us -> 141 us  [on_device(): pl.pallas_call(functools.partial(kernel, n, n_az, margin_blocks, groups,...]
where the time goes in v2:
time: 143 us
  Pallas kernels  141 us (99%)
  local copies, waits for them, and re-layouts  2.67 us (2%)
    pallas_call x1, Pallas kernels, on_device(): pl.pallas_call(functools.partial(kernel, n, n_az, margin_blocks, groups,...  141 us

profile of v2, /device:TPU:0, one launch (start us, length us, event | category | flops | bytes accessed | tf_op | source)
XLA Modules:
  0.0 143.3 jit_solution(12444601754529318653)
XLA Ops:
  0.0 140.6 %shard_map.82 = bf16[768,1024]{1,0:T(8,128)(2,1)} custom-call(bf16[48,16384]{1,0:T(8,128)(2,1)} %bitcast.3, bf16[32,16384]{1,0:T(8,128)(2,1)} %scaling.1, bf16[32,16384]{1,0:T(8,128)(2,1)} %rng.1, bf16[32,16384]{1,0:T(8,128)(2,1)} %residual.1, bf16[4,256,1056]{2,1,0:T(8,128)(2,1)} %constant.8.clone.forward_in, ...), custom_call_target="tpu_custom_call" | custom-call | tf_op jit(solution)/shard_map/pallas_call | solution.py:415
  140.6 2.7 %copy.10 = bf16[2,384,1024]{2,1,0:T(8,128)(2,1)} copy(bf16[2,384,1024]{2,1,0:T(8,128)(2,1)} %bitcast.2) | data formatting | bytes 3145728

commit v3 on v1

--- a/solution.py
+++ b/solution.py
@@ -136,11 +136,8 @@
             for j in range(margin_blocks):
                 recv1[ch, n + j] = jnp.zeros(recv1.shape[2:], BF16)
 
-    def natural_table(k, table):
-        loads[k].wait()
-
-        def natural(step, carry):
-            pair, d = lax.div(step, n), lax.rem(step, n)
+    def natural_table(k, table, pair):
+        def natural(d, carry):
             rows = pl.ds(pl.multiple_of(pair * 2 * FG, 2 * FG), 2 * FG)
             c, s = cos_sin(ph[k, rows, columns(d)].astype(F32))
             for h in range(2):
@@ -148,7 +145,7 @@
                 table[2 * pair + h, d, 1] = s[h * FG : (h + 1) * FG]
             return carry
 
-        lax.fori_loop(0, n * (groups // 2), natural, 0)
+        lax.fori_loop(0, n, natural, 0)
 
     def turned_table():
         loads[1].wait()
@@ -229,18 +226,25 @@
                 forward[g], recv1[ch].reshape(depth, cw), preferred_element_type=F32
             )
             spec[g, ch] = total.astype(BF16).reshape(n, 2 * FG, cw)
-            send_group(spec, recv2, (g, ch), s2, r2, l2)
+
+            @pl.when((g == 0) if ch == 0 else (g > 0))
+            def _():
+                send_group(spec, recv2, (g, 0), s2, r2, l2)
+
+            if ch == 1:
+                send_group(spec, recv2, (g, 1), s2, r2, l2)
             return carry
 
         lax.fori_loop(0, groups, azimuth, 0)
 
-    natural_table(0, sc_t)
+    loads[0].wait()
+    for pair in range(groups // 2):
+        natural_table(0, sc_t, pair)
     loads[3].wait()
     azimuth_chunk(0)
     turned_table()
     azimuth_chunk(1)
-    natural_table(2, rs_t)
-    for k in (4, 5, 6):
+    for k in (2, 4, 5, 6):
         loads[k].wait()
 
     def part(values, f):
@@ -314,7 +318,11 @@
         send_group(send3, recv3, (g,), s3, r3, l3)
         return carry
 
-    lax.fori_loop(0, groups, range_group, 0)
+    def range_pair(pair, carry):
+        natural_table(2, rs_t, pair)
+        return lax.fori_loop(2 * pair, 2 * pair + 2, range_group, carry)
+
+    lax.fori_loop(0, groups // 2, range_pair, 0)
 
     for g in range(groups):
         group_arrived(send3, recv3, (g,), r3, l3)

time: 137 us -> 137 us (level)
  no operation moved by 1% of the time
where the time goes in v3:
time: 137 us
  Pallas kernels  134 us (98%)
  local copies, waits for them, and re-layouts  2.67 us (2%)
    pallas_call x1, Pallas kernels, on_device(): pl.pallas_call(functools.partial(kernel, n, n_az, margin_blocks, groups,...  134 us

profile of v3, /device:TPU:0, one launch (start us, length us, event | category | flops | bytes accessed | tf_op | source)
XLA Modules:
  0.0 136.9 jit_solution(2385805823693751157)
XLA Ops:
  0.0 134.2 %shard_map.82 = bf16[768,1024]{1,0:T(8,128)(2,1)} custom-call(bf16[48,16384]{1,0:T(8,128)(2,1)} %bitcast.3, bf16[32,16384]{1,0:T(8,128)(2,1)} %scaling.1, bf16[32,16384]{1,0:T(8,128)(2,1)} %rng.1, bf16[32,16384]{1,0:T(8,128)(2,1)} %residual.1, bf16[4,256,1056]{2,1,0:T(8,128)(2,1)} %constant.8.clone.forward_in, ...), custom_call_target="tpu_custom_call" | custom-call | tf_op jit(solution)/shard_map/pallas_call | solution.py:369
  134.2 2.7 %copy.10 = bf16[2,384,1024]{2,1,0:T(8,128)(2,1)} copy(bf16[2,384,1024]{2,1,0:T(8,128)(2,1)} %bitcast.2) | data formatting | bytes 3145728
